TPU v7x, 1024 devices: a whole 4x8x16 slice. The times are simulated.
1024 devices in a mesh: ctx: 64 (over z, x), ep: 16 (over y, core).
Axes of the slice: x: 4, y: 8, z: 16, core: 2. Of those that a mesh axis runs over, the one named last changes fastest.
Arguments:
- grad_out: bfloat16 [8192, 6144], P('ctx', 'ep'), may hold values from -24 to 24
- logits: float32 [8192, 16], P('ctx'), may hold values from -8 to 270
- expert_ids: int32 [8192, 4], P('ctx'), may hold values from 0 to 15, as said below
- hidden_act: bfloat16 [10752, 3328], P('ctx'), may hold values from -1.5 to 1.5
- down_weight: bfloat16 [10752, 6144], P('ctx', 'ep'), may hold values from -0.0625 to 0.0625
- router_weight: float32 [6144, 16], P('ep'), may hold values from -0.3 to 0.3
Outputs:
- grad_down: bfloat16 [10752, 6144], P('ctx', 'ep')
- grad_hidden: bfloat16 [10752, 3328], P('ctx', 'ep')
- grad_tokens: bfloat16 [8192, 6144], P('ctx', 'ep')
Inputs may be any that keep to these rules, and one draw needn't show every extreme that they name: `expert_ids`: each token names 4 different experts. Within each block of 128 tokens (the tokens of one index of ctx) the tokens that name expert 0 number at least a quarter of 52, rounded down, and at most 52, and in every draw some block has exactly 52 of them.
All inputs are finite; a program needn't handle non-finite values.
Results may differ from a plain program's by a relative error of at most 0.0057.
Values may be sent and summed in bfloat16 or wider, within the bound.
A program may use at most 32 MiB of HBM per device.

v0:
```python
import jax
import jax.numpy as jnp
from jax import lax
from jax.sharding import PartitionSpec as P

CAP = 52


def shards(grad_out, logits, expert_ids, hidden_act, down_weight, router_weight):
    tokens_here, width_here = grad_out.shape
    experts = logits.shape[1]
    router_probs = jax.nn.softmax(logits, axis=-1)
    is_named = jnp.any(expert_ids == 0, axis=1)
    route_weight = jnp.where(is_named, router_probs[:, 0], 0.0).astype(jnp.bfloat16)
    named_count = is_named.astype(jnp.float32)
    slot_pos = (jnp.cumsum(named_count) - named_count).astype(jnp.int32)
    select = jnp.where(
        is_named[None, :] & (slot_pos[None, :] == lax.iota(jnp.int32, CAP)[:, None]), 1.0, 0.0
    ).astype(jnp.float32)
    slot_tag = jnp.where(is_named, slot_pos.astype(jnp.float32) + 1.0, 0.0).astype(jnp.bfloat16)
    token_rows = lax.all_gather(grad_out, "ctx", axis=0, tiled=True)
    token_prob = lax.all_gather(route_weight, "ctx", axis=0, tiled=True)
    token_tag = lax.all_gather(slot_tag, "ctx", axis=0, tiled=True)
    sources = token_rows.shape[0] // tokens_here
    token_rows = token_rows.reshape(sources, tokens_here, width_here)
    prob_float = token_prob.astype(jnp.float32).reshape(sources, tokens_here)
    tag_float = token_tag.astype(jnp.float32).reshape(sources, tokens_here)
    wanted = (lax.iota(jnp.int32, CAP) + 1).astype(jnp.float32)
    picked = jnp.where(tag_float[:, None, :] == wanted[None, :, None], 1.0, 0.0).astype(jnp.float32)
    slot_rows = (
        jnp.einsum(
            "sjt,std->sjd",
            picked.astype(jnp.bfloat16),
            token_rows,
            preferred_element_type=jnp.float32,
        )
        .astype(jnp.bfloat16)
        .reshape(sources * CAP, width_here)
    )
    slot_prob = (
        jnp.einsum("sjt,st->sj", picked, prob_float, precision=lax.Precision.HIGHEST)
        .astype(jnp.bfloat16)
        .reshape(sources * CAP)
    )
    prob_column = slot_prob.astype(jnp.float32)
    scaled = (prob_column[:, None] * slot_rows.astype(jnp.float32)).astype(jnp.bfloat16)
    grad_sum = jnp.dot(hidden_act, scaled, preferred_element_type=jnp.float32)
    backward = lax.dot_general(
        slot_rows, down_weight, (((1,), (1,)), ((), ())), preferred_element_type=jnp.float32
    )
    partial_back = backward
    slot_weights = prob_column
    running = (grad_sum, partial_back, slot_weights)
    grad_sum, partial_back, slot_weights = running
    backward = lax.psum_scatter(partial_back, "ep", scatter_dimension=0, tiled=True)
    share_rows = backward.shape[0]
    first_share = lax.axis_index("ep") * share_rows
    share_weights = lax.dynamic_slice_in_dim(slot_weights, first_share, share_rows, 0)
    grad_hidden = (share_weights[:, None] * backward).astype(jnp.bfloat16).T
    hidden_share = lax.dynamic_slice_in_dim(hidden_act, first_share, share_rows, 1)
    partial_score = jnp.sum(hidden_share.astype(jnp.float32).T * backward, axis=1)
    share_score = lax.psum(partial_score, "ctx")
    slot_score = lax.all_gather(share_score, "ep", axis=0, tiled=True)
    own_scores = lax.dynamic_slice_in_dim(slot_score, lax.axis_index("ctx") * CAP, CAP, 0)
    route_grad = jnp.dot(own_scores, select, precision=lax.Precision.HIGHEST)
    spread = jnp.where(lax.iota(jnp.int32, experts)[None, :] == 0, route_grad[:, None], 0.0)
    logit_grad = router_probs * (spread - jnp.sum(router_probs * spread, axis=1, keepdims=True))
    grad_tokens = lax.dot_general(
        logit_grad, router_weight, (((1,), (1,)), ((), ())), precision=lax.Precision.HIGHEST
    ).astype(jnp.bfloat16)
    return (grad_sum.astype(jnp.bfloat16), grad_hidden, grad_tokens)


def solution(mesh):
    placed = (
        P("ctx", "ep"),
        P("ctx", None),
        P("ctx", None),
        P("ctx", None),
        P("ctx", "ep"),
        P("ep", None),
    )
    return jax.shard_map(
        shards,
        mesh=mesh,
        in_specs=placed,
        out_specs=(P("ctx", "ep"), P("ctx", "ep"), P("ctx", "ep")),
        check_vma=False,
    )
```

profile of v0, /device:TPU:2, one launch (start us, length us, event | category | flops | bytes accessed | tf_op | source)
XLA Modules:
  0.0 531.7 jit_solution(17022395701607625848)
XLA Ops:
  7.2 0.0 copy-start
  7.2 0.0 all-gather.4.cloned.1.call-start
  7.2 0.7 all-gather.4.cloned.1.call-update
  7.9 0.0 reduce-scatter.4.cloned.1.call-start
  8.0 0.7 compare_reduce_fusion
  8.7 0.1 copy.11
  8.8 0.2 reduce-window.7
  9.0 0.1 reduce
  9.1 86.2 %all-gather = bf16[64,1,128]{2,1,0:T(2,128)(2,1)S(1)} all-gather(bf16[1,1,128]{2,1,0:T(2,128)(2,1)S(1)} %get-tuple-element.5), channel_id=1, replica_groups=mesh['ctx'=64,'ep'=16] {'ctx'}, dimensions={0}, use_global_device_ids=true | all-gather | bytes 16640 | tf_op jit(solution)/shard_map/all_gather | solution.py:23
  95.3 82.2 %all-gather.4.cloned.1.call-done = bf16[8192,384]{1,0:T(8,128)(2,1)} async-done(((bf16[128,384]{1,0:T(8,128)(2,1)}), bf16[8192,384]{1,0:T(8,128)(2,1)}) %all-gather.4.cloned.1.call-update) | async-done | bytes 6291472 | tf_op jit(solution)/shard_map/all_gather | solution.py:21
  177.5 5.7 %convolution_convert_fusion = bf16[64,52,384]{2,1,0:T(8,128)(2,1)} fusion(bf16[64,128,384]{2,1,0:T(8,128)(2,1)} %bitcast.41, f32[64,128]{1,0:T(8,128)S(1)} %bitcast.42, f32[52]{0:T(128)S(1)} %add_convert_fusion), kind=kOutput, calls=%fused_computation.7 | convolution fusion | flops 329711616 | bytes 8880336 | tf_op jit(solution)/shard_map/sjt,std->sjd/dot_general | solution.py:31
  183.2 3.5 reshape.73
  186.7 0.0 copy-done
  186.7 2.8 fusion.49
  189.5 0.0 copy-start.1
  189.5 0.0 reduce-scatter.4.cloned.1.call-update
  189.5 1.3 dynamic-slice
  191.4 0.0 copy-done.1
  191.5 62.6 %reduce-scatter.4.cloned.1.call-done = f32[208,168]{1,0:T(8,128)} async-done(((f32[3328,168]{1,0:T(8,128)}), f32[208,168]{1,0:T(8,128)}) %reduce-scatter.4.cloned.1.call-update) | async-done | bytes 139792
  254.1 1.0 copy.15
  255.2 1.0 fusion.15
  256.2 141.7 %psum.7 = f32[208]{0:T(256)S(1)} all-reduce(f32[208]{0:T(256)S(1)} %fusion.15), channel_id=1, replica_groups=mesh['ctx'=64,'ep'=16] {'ctx'}, use_global_device_ids=true, to_apply=%region_6.7 | all-reduce | flops 208 | bytes 1664 | tf_op jit(solution)/shard_map/psum | solution.py:62
  397.9 0.3 dynamic-update-slice
  398.2 45.7 %all-reduce = f32[3328]{0:T(1024)S(1)} all-reduce(f32[3328]{0:T(1024)S(1)} %dynamic-update-slice), channel_id=1, replica_groups=mesh['ctx'=64,'ep'=16] {'ep'}, use_global_device_ids=true, to_apply=%add | all-reduce | flops 3328 | bytes 26624
  443.9 0.2 convolution_bitcast_fusion
  444.1 0.1 fusion.25
  444.2 74.4 %all-gather.1 = bf16[64,1,128]{2,1,0:T(2,128)(2,1)S(1)} all-gather(bf16[1,1,128]{2,1,0:T(2,128)(2,1)S(1)} %fusion.36), channel_id=1, replica_groups=mesh['ctx'=64,'ep'=16] {'ctx'}, dimensions={0}, use_global_device_ids=true | all-gather | bytes 16640 | tf_op jit(solution)/shard_map/all_gather | solution.py:22
  518.6 1.6 fusion.2
  520.2 0.1 reshape.76
  520.3 0.0 copy-start.2
  520.3 2.8 fusion.6
  523.1 0.1 dynamic_slice.9
  523.2 0.7 fusion.16
  523.8 0.0 copy-done.2
  523.8 1.1 convolution_convert_fusion.1
  (10 shorter events, 0.1 us)
Async XLA Ops:
  7.2 179.5 %copy-start = (bf16[168,384]{1,0:T(8,128)(2,1)S(1)}, bf16[168,384]{1,0:T(8,128)(2,1)}, u32[]{:S(2)}) copy-start(bf16[168,384]{1,0:T(8,128)(2,1)} %param.10) | copy-start | bytes 387076
  7.2 170.4 %all-gather.4.cloned.1.call-start = ((), (), s32[]{:S(2)}) async-start(), calls=%async_computation.1 | async-start | bytes 6389760 | tf_op jit(solution)/shard_map/all_gather | solution.py:21
  7.9 246.2 %reduce-scatter.4.cloned.1.call-start = ((), (), s32[]{:S(2)}) async-start(), calls=%async_computation.2 | async-start | bytes 3620864
  189.5 2.0 copy-start.1
  520.3 3.5 copy-start.2
Sparse Core Ops, SparseCore 0:
  12.1 165.3 all-gather.3
  189.6 64.4 reduce-scatter.3
where the time goes:
time: 532 us
  blocking collectives  348 us (65%)
  waiting for transfers between devices  146 us (27%)
  between operations  14.8 us (3%)
  matrix products  14.1 us (3%)
  local copies, waits for them, and re-layouts  6.36 us (1%)
    psum x1, blocking collectives, shards(): share_score = lax.psum(partial_score, 'ctx')  142 us
    all_gather x1, blocking collectives, shards(): token_tag = lax.all_gather(slot_tag, 'ctx', axis=0, tiled=True)  86.2 us
    all_gather x1, waiting for transfers between devices, shards(): token_rows = lax.all_gather(grad_out, 'ctx', axis=0, tiled=True)  82.2 us
    all_gather x1, blocking collectives, shards(): token_prob = lax.all_gather(route_weight, 'ctx', axis=0, tiled=True)  74.4 us
    unnamed x3, waiting for transfers between devices  63.3 us
    unnamed x1, blocking collectives  45.7 us
  transfers between devices with their start and end apart: 2, of which 2 were waited for; matrix products, arithmetic and copies ran while one was open for 0% of the time, Pallas kernels for 0%

commit v1 on v0

v1 whole, which is shorter than its diff:
```python
import functools

import jax
import jax.numpy as jnp
from jax import lax
from jax.experimental import pallas as pl
from jax.experimental.pallas import tpu as pltpu
from jax.sharding import PartitionSpec as P

MESH = pl.DeviceIdType.MESH
CAP = 52
NZ, NX, NY = 16, 4, 8
DZ = (0, 1, -1, 3, -3, 2, -2, 4, -4, 6, -6, 5, -5, 7, -7, 8)
AT = {d: i for i, d in enumerate(DZ)}
AT[-8] = AT[8]
GROUPS = ((0, 5), (5, 11), (11, 16))
HAND_ON = {
    0: (3, -3, 1, -1),
    -3: (3, 1, -1),
    3: (-3, 1, -1),
    -6: (1, -1, 2),
    6: (1, -1),
}
F32, BF16 = jnp.float32, jnp.bfloat16


def pick(index, table):
    out = jnp.int32(table[0])
    for i, v in enumerate(table):
        if i:
            out = jnp.where(index == i, jnp.int32(v), out)
    return out


def kernel(
    grad_out, logits_t, ids_t, hidden, down, router_t,
    grad_down, grad_hidden, grad_tokens,
    go_v, log_v, ids_v, hid_v, down_v, rw_v,
    hp, wp, abuf, bbuf, acc, own, pbuf, sib, comb, rsb, wshare,
    sc, s1, s2s, s2, s3s, s3, s4s, s4, sel_t, qmat,
    in_sem, ax_s, ax_r, az_s, az_r, bz_s, bz_r, bx_s, bx_r,
    sib_s, sib_r, y_s, y_r, s1_s, s1_r, s2_s, s2_r, s3_s, s3_r, s4_s, s4_r,
):
    ctx, ep = lax.axis_index("ctx"), lax.axis_index("ep")
    z, x = ctx // NX, lax.rem(ctx, NX)
    y, core = ep // 2, lax.rem(ep, 2)

    def at_z(d):
        return (lax.rem(z + d + NZ, NZ) * NX + x, ep)

    def at_x(d):
        return (z * NX + lax.rem(x + d, NX), ep)

    def at_y(d):
        return (ctx, lax.rem(y + d, NY) * 2 + core)

    sibling = (ctx, y * 2 + 1 - core)

    def remote(src, dst, send, recv, to):
        return pltpu.make_async_remote_copy(
            src_ref=src, dst_ref=dst, send_sem=send, recv_sem=recv, device_id=to, device_id_type=MESH
        )

    loads = [
        pltpu.make_async_copy(s, d, in_sem.at[i])
        for i, (s, d) in enumerate(
            ((ids_t, ids_v), (grad_out, go_v), (logits_t, log_v), (hidden, hid_v), (down, down_v), (router_t, rw_v))
        )
    ]
    for c in loads:
        c.start()

    barrier = pltpu.get_barrier_semaphore()
    greet = [at_z(d) for d in (1, -1, 2, -2, 3, -3)] + [at_x(d) for d in (1, 2, 3)]
    greet += [at_y(d) for d in range(1, NY)] + [sibling]
    for to in greet:
        pl.semaphore_signal(barrier, inc=1, device_id=to, device_id_type=MESH)

    loads[0].wait()
    named = jnp.max(jnp.where(ids_v[...] == 0, 1.0, 0.0).astype(F32), axis=0, keepdims=True)
    rows = lax.broadcasted_iota(jnp.int32, (128, 128), 0)
    cols = lax.broadcasted_iota(jnp.int32, (128, 128), 1)
    before = jnp.where(rows < cols, 1.0, 0.0).astype(BF16)
    named8 = jnp.broadcast_to(named, (8, 128))
    pos = jnp.dot(named8.astype(BF16), before, preferred_element_type=F32)[0:1]
    slot_row = lax.rem(rows, 64).astype(F32)
    sel = jnp.where((slot_row == pos) & (named > 0.5), 1.0, 0.0).astype(F32)
    sel_bf = sel.astype(BF16)

    loads[2].wait()
    logit = log_v[...]
    grown = jnp.exp(logit - jnp.max(logit, axis=0, keepdims=True))
    probs = grown / jnp.sum(grown, axis=0, keepdims=True)
    p0 = probs[0:1]
    weight = jnp.where(named > 0.5, p0, 0.0).astype(BF16)
    weight_row = lax.dot_general(
        jnp.broadcast_to(weight.astype(F32), (8, 128)).astype(BF16), sel_bf,
        (((1,), (1,)), ((), ())), preferred_element_type=F32,
    )[0:1]

    loads[1].wait()
    slots = jnp.dot(sel_bf[0:64], go_v[...], preferred_element_type=F32)
    row64 = lax.broadcasted_iota(jnp.int32, (64, 128), 0)
    abuf[0, x] = jnp.where(row64 == CAP, weight_row, slots[:, 0:128]).astype(BF16)
    bbuf[x, 0] = jnp.concatenate([slots[0:56, 128:256], slots[0:56, 256:384]], axis=0).astype(BF16)

    pl.semaphore_wait(barrier, len(greet))

    sends = []

    def start(c):
        c.start()
        sends.append(c)

    ax_in = []
    for d in (1, 3, 2):
        start(remote(abuf.at[0, x], abuf.at[0, x], ax_s.at[d], ax_r.at[d], at_x(d)))

    az_in, bz_in = {}, {}

    def hand_on(buf_of, d, send, recv, into, base):
        for i, shift in enumerate(HAND_ON[d]):
            there = AT[d - shift]
            c = remote(buf_of(AT[d]), buf_of(there), send.at[base + i], recv.at[there], at_z(shift))
            start(c)
            into[there] = c

    bases = {0: 0, -3: 4, 3: 7, -6: 10, 6: 13}

    def send_a(d):
        hand_on(lambda i: abuf.at[i], d, az_s, az_r, az_in, bases[d])

    def send_b(d):
        hand_on(lambda i: bbuf.at[x, i], d, bz_s, bz_r, bz_in, bases[d])

    def wait_a(d):
        i = AT[d]
        remote(abuf.at[i], abuf.at[i], az_s.at[0], az_r.at[i], at_z(1)).wait_recv()

    def wait_b(d):
        i = AT[d]
        remote(bbuf.at[x, i], bbuf.at[x, i], bz_s.at[0], bz_r.at[i], at_z(1)).wait_recv()

    def send_bx(g):
        lo, hi = GROUPS[g]
        for d in (1, 3, 2):
            block = bbuf.at[x, pl.ds(lo, hi - lo)]
            start(remote(block, block, bx_s.at[g, d], bx_r.at[g, d], at_x(d)))

    def wait_bx(g):
        lo, hi = GROUPS[g]
        for d in (1, 3, 2):
            block = bbuf.at[lax.rem(x + NX - d, NX), pl.ds(lo, hi - lo)]
            remote(block, block, bx_s.at[g, d], bx_r.at[g, d], at_x(d)).wait_recv()

    send_b(0)

    loads[4].wait()
    zero8 = jnp.zeros((8, 384), F32)
    wp[...] = jnp.concatenate([down_v[...].astype(F32), zero8], axis=0).astype(BF16)
    loads[3].wait()

    def spread(e, _):
        first = e * (NX * CAP)
        tile = jnp.minimum(first // 128, 23)
        off = first - tile * 128
        r = lax.broadcasted_iota(jnp.int32, (384, 256), 0)
        c = lax.broadcasted_iota(jnp.int32, (384, 256), 1)
        lane = lax.rem(c, 64)
        move = jnp.where((r == off + (c // 64) * CAP + lane) & (lane < CAP), 1.0, 0.0).astype(BF16)
        out = jnp.dot(hid_v[:, pl.ds(pl.multiple_of(tile * 128, 128), 384)], move, preferred_element_type=F32)
        hp[e] = jnp.concatenate([out, jnp.zeros((8, 256), F32)], axis=0).astype(BF16)
        return 0

    lax.fori_loop(0, 6, spread, 0)

    for d in (1, 3, 2):
        block = abuf.at[0, lax.rem(x + NX - d, NX)]
        remote(block, block, ax_s.at[d], ax_r.at[d], at_x(d)).wait_recv()
    send_a(0)

    lax.fori_loop(6, 16, spread, 0)
    acc[...] = jnp.zeros_like(acc)

    wait_b(-3)
    send_b(-3)
    wait_b(3)
    send_b(3)
    wait_b(1)
    wait_b(-1)
    send_bx(0)
    wait_a(-3)
    send_a(-3)
    wait_a(3)
    send_a(3)

    sel_t[...] = sel.T
    loads[5].wait()
    slope = probs * (jnp.where(lax.broadcasted_iota(jnp.int32, (16, 128), 0) == 0, 1.0, 0.0) - p0)
    qmat[...] = lax.dot_general(
        slope, rw_v[...], (((0,), (0,)), ((), ())), precision=lax.Precision.HIGHEST, preferred_element_type=F32
    )

    wait_b(-6)
    send_b(-6)
    wait_b(6)
    send_b(6)
    for d in (2, -2, 4, -4):
        wait_b(d)
    send_bx(1)
    wait_a(-6)
    send_a(-6)
    wait_a(6)
    send_a(6)

    lane128 = lax.broadcasted_iota(jnp.int32, (1, 128), 1)
    row8 = lax.broadcasted_iota(jnp.int32, (8, 128), 0)

    def share_of(i):
        return lax.rem(z + pick(i, DZ) + NZ, NZ)

    def to_owner(i):
        e = share_of(i)
        return remote(sc.at[i], s1.at[i], s1_s.at[i], s1_r.at[i], (e * NX + x, ep))

    def to_sibling(i):
        return remote(pbuf.at[i], sib.at[i], sib_s.at[i], sib_r.at[i], sibling)

    def to_share(i):
        e = share_of(i)
        return remote(comb.at[i], rsb.at[y], y_s.at[i], y_r.at[y], (ctx, e))

    def add_pair(i):
        e = share_of(i)

        @pl.when(lax.rem(e, 2) == core)
        def _():
            to_sibling(i).wait_recv()
            both = (own[lax.rem(i, 2)] + sib[i].astype(F32)).astype(BF16)

            @pl.when(e == ep)
            def _():
                rsb[y] = both

            @pl.when(e != ep)
            def _():
                comb[i] = both
                to_share(i).start()

    def chunk(i, _):
        e = share_of(i)
        a = [abuf[i, k].astype(F32) for k in range(NX)]
        b = [bbuf[k, i].astype(F32) for k in range(NX)]
        pad = jnp.zeros((8, 128), F32)
        g0 = jnp.concatenate(a, axis=0).astype(BF16)
        g1 = jnp.concatenate([v for k in range(NX) for v in (b[k][0:56], pad)], axis=0).astype(BF16)
        g2 = jnp.concatenate([v for k in range(NX) for v in (b[k][56:112], pad)], axis=0).astype(BF16)
        g = jnp.concatenate([g0, g1, g2], axis=1)
        w = jnp.concatenate(
            [jnp.where(lane128 < 64, a[k][CAP:CAP + 1], a[k + 1][CAP:CAP + 1]) for k in (0, 2)], axis=1
        )
        h = hp[e].astype(F32)
        back = lax.dot_general(wp[...], g, (((1,), (1,)), ((), ())), preferred_element_type=F32)
        score = jnp.sum(h * back, axis=0, keepdims=True)
        both_rows = jnp.where(row8 == 0, score[:, 0:128], jnp.where(row8 == 1, score[:, 128:256], 0.0))

        @pl.when(i == 0)
        def _():
            s1[0] = both_rows

        @pl.when(i != 0)
        def _():
            sc[i] = both_rows
            to_owner(i).start()

        @pl.when(lax.rem(e, 2) == core)
        def _():
            own[lax.rem(i, 2)] = back

        @pl.when(lax.rem(e, 2) != core)
        def _():
            pbuf[i] = back.astype(BF16)
            to_sibling(i).start()

        @pl.when(e == ep)
        def _():
            wshare[...] = jnp.broadcast_to(w, (8, 256))

        acc[...] += jnp.dot((h * w).astype(BF16), g, preferred_element_type=F32)

        @pl.when(i != 0)
        def _():
            add_pair(i - 1)

        return 0

    for d in (1, -1):
        wait_a(d)
    wait_bx(0)
    lax.fori_loop(0, 2, chunk, 0)
    for d in (5, -5, 7, -7, 8):
        wait_b(d)
    send_bx(2)
    lax.fori_loop(2, 5, chunk, 0)
    for d in (2, -2, 4, -4):
        wait_a(d)
    wait_bx(1)
    lax.fori_loop(5, 11, chunk, 0)
    for d in (5, -5, 7, -7, 8):
        wait_a(d)
    wait_bx(2)
    lax.fori_loop(11, 16, chunk, 0)
    add_pair(15)

    def s1_wait(i, _):
        to_owner(i).wait_recv()
        return 0

    grad_down[...] = acc[0:168].astype(BF16)
    lax.fori_loop(1, 16, s1_wait, 0)
    s2s[...] = jnp.sum(s1[...], axis=0)
    for d in (1, 3, 2):
        start(remote(s2s, s2.at[d], s2_s.at[d], s2_r.at[d], at_x(d)))
    s2[0] = s2s[...]
    for d in (1, 3, 2):
        remote(s2s, s2.at[d], s2_s.at[d], s2_r.at[d], at_x(d)).wait_recv()
    s3s[...] = jnp.sum(s2[...], axis=0)
    for d in range(1, NY):
        start(remote(s3s, s3.at[d], s3_s.at[d], s3_r.at[d], at_y(d)))
    s3[0] = s3s[...]

    for d in range(1, NY):
        src = lax.rem(y + NY - d, NY)
        remote(rsb.at[src], rsb.at[src], y_s.at[0], y_r.at[src], sibling).wait_recv()
    total = rsb[0].astype(F32)
    for d in range(1, NY):
        total = total + rsb[d].astype(F32)
    total = total * wshare[0:1]
    grad_hidden[...] = jnp.concatenate(
        [total[0:168, 64 * k:64 * k + CAP] for k in range(NX)], axis=1
    ).astype(BF16)

    for d in range(1, NY):
        remote(s3s, s3.at[d], s3_s.at[d], s3_r.at[d], at_y(d)).wait_recv()
    s4s[...] = jnp.sum(s3[...], axis=0)
    start(remote(s4s, s4, s4_s.at[0], s4_r.at[0], sibling))
    remote(s4s, s4, s4_s.at[0], s4_r.at[0], sibling).wait_recv()
    scores = s4s[...] + s4[...]
    row = jnp.where(x >= 2, scores[1:2], scores[0:1])
    row = jnp.where(lane128 // 64 == lax.rem(x, 2), row, 0.0)
    route = jnp.sum(sel_t[...] * row, axis=1, keepdims=True)
    grad_tokens[...] = (route * qmat[...]).astype(BF16)

    for c in sends:
        c.wait_send()

    def drain(i, _):
        @pl.when(i != 0)
        def _():
            to_owner(i).wait_send()

        e = share_of(i)

        @pl.when(lax.rem(e, 2) != core)
        def _():
            to_sibling(i).wait_send()

        @pl.when((lax.rem(e, 2) == core) & (e != ep))
        def _():
            to_share(i).wait_send()

        return 0

    lax.fori_loop(0, 16, drain, 0)


def shards(grad_out, logits, expert_ids, hidden_act, down_weight, router_weight):
    dma = pltpu.SemaphoreType.DMA
    ng = len(GROUPS)
    return pl.pallas_call(
        kernel,
        out_shape=(
            jax.ShapeDtypeStruct((168, 384), BF16),
            jax.ShapeDtypeStruct((168, 208), BF16),
            jax.ShapeDtypeStruct((128, 384), BF16),
        ),
        in_specs=[pl.BlockSpec(memory_space=pl.ANY)] * 6,
        out_specs=[pl.BlockSpec(memory_space=pltpu.VMEM)] * 3,
        scratch_shapes=[
            pltpu.VMEM((128, 384), BF16),
            pltpu.VMEM((16, 128), F32),
            pltpu.VMEM((4, 128), jnp.int32),
            pltpu.VMEM((168, 3328), BF16),
            pltpu.VMEM((168, 384), BF16),
            pltpu.VMEM((16, 384), F32),
            pltpu.VMEM((16, 176, 256), BF16),
            pltpu.VMEM((176, 384), BF16),
            pltpu.VMEM((16, NX, 64, 128), BF16),
            pltpu.VMEM((NX, 16, 112, 128), BF16),
            pltpu.VMEM((176, 384), F32),
            pltpu.VMEM((2, 176, 256), F32),
            pltpu.VMEM((16, 176, 256), BF16),
            pltpu.VMEM((16, 176, 256), BF16),
            pltpu.VMEM((16, 176, 256), BF16),
            pltpu.VMEM((NY, 176, 256), BF16),
            pltpu.VMEM((8, 256), F32),
            pltpu.VMEM((16, 8, 128), F32),
            pltpu.VMEM((16, 8, 128), F32),
            pltpu.VMEM((8, 128), F32),
            pltpu.VMEM((NX, 8, 128), F32),
            pltpu.VMEM((8, 128), F32),
            pltpu.VMEM((NY, 8, 128), F32),
            pltpu.VMEM((8, 128), F32),
            pltpu.VMEM((8, 128), F32),
            pltpu.VMEM((128, 128), F32),
            pltpu.VMEM((128, 384), F32),
            dma((6,)),
            dma((NX,)), dma((NX,)),
            dma((15,)), dma((16,)),
            dma((15,)), dma((16,)),
            dma((ng, NX)), dma((ng, NX)),
            dma((16,)), dma((16,)),
            dma((16,)), dma((NY,)),
            dma((16,)), dma((16,)),
            dma((NX,)), dma((NX,)),
            dma((NY,)), dma((NY,)),
            dma((1,)), dma((1,)),
        ],
        compiler_params=pltpu.CompilerParams(
            collective_id=0, has_side_effects=True, vmem_limit_bytes=48 << 20
        ),
    )(grad_out, logits.T, expert_ids.T, hidden_act, down_weight, router_weight.T)


def solution(mesh):
    placed = (
        P("ctx", "ep"),
        P("ctx", None),
        P("ctx", None),
        P("ctx", None),
        P("ctx", "ep"),
        P("ep", None),
    )
    return jax.shard_map(
        shards,
        mesh=mesh,
        in_specs=placed,
        out_specs=(P("ctx", "ep"), P("ctx", "ep"), P("ctx", "ep")),
        check_vma=False,
    )
```

time: 532 us -> 82.3 us (0.15)
  the two profiles are of different devices: /device:TPU:2 before, /device:TPU:1 now
where the time goes in v1:
time: 82.3 us; the launch traced here: 82 us
  Pallas kernels  74.2 us (90%)
  local copies, waits for them, and re-layouts  7.08 us (9%)
    pallas_call x1, Pallas kernels, shards(): pl.pallas_call(kernel, out_shape=(jax.ShapeDtypeStruct((168, 384), BF16),...  74.2 us
    unnamed x15, local copies, waits for them, and re-layouts  7.08 us

profile of v1, /device:TPU:1, one launch (start us, length us, event | category | flops | bytes accessed | tf_op | source)
XLA Modules:
  0.0 82.0 jit_solution(15885935050109051478)
XLA Ops:
  0.6 0.0 copy-start
  0.6 1.2 %copy-done = bf16[168,3328]{1,0:T(8,128)(2,1)S(1)} copy-done((bf16[168,3328]{1,0:T(8,128)(2,1)S(1)}, bf16[168,3328]{1,0:T(8,128)(2,1)}, u32[]{:S(2)}) %copy-start) | copy-done | bytes 1118232
  1.9 0.0 copy-start.1
  1.9 0.9 %copy-done.1 = bf16[168,384]{1,0:T(8,128)(2,1)S(1)} copy-done((bf16[168,384]{1,0:T(8,128)(2,1)S(1)}, bf16[168,384]{1,0:T(8,128)(2,1)}, u32[]{:S(2)}) %copy-start.1) | copy-done | bytes 129048
  2.8 0.0 copy-start.2
  2.8 0.9 %copy-done.2 = bf16[128,384]{1,0:T(8,128)(2,1)S(1)} copy-done((bf16[128,384]{1,0:T(8,128)(2,1)S(1)}, bf16[128,384]{1,0:T(8,128)(2,1)}, u32[]{:S(2)}) %copy-start.2) | copy-done | bytes 98328
  3.7 0.0 copy-start.3
  3.7 0.7 copy-done.3
  4.4 0.0 copy-start.4
  4.4 0.7 copy-done.4
  5.1 0.0 copy-start.5
  5.1 0.7 copy-done.5
  5.8 74.2 %shard_map.85 = (bf16[168,384]{1,0:T(8,128)(2,1)S(1)}, bf16[168,208]{1,0:T(8,128)(2,1)S(1)}, bf16[128,384]{1,0:T(8,128)(2,1)S(1)}) custom-call(bf16[128,384]{1,0:T(8,128)(2,1)S(1)} %copy-done.2, f32[16,128]{1,0:T(8,128)S(1)} %bitcast.4, s32[4,128]{1,0:T(4,128)S(1)} %bitcast.5, bf16[168,3328]{1,0:T(8,128)(2,1)S(1)} %copy-done, ...), custom_call_target="tpu_custom_call" | custom-call | tf_op jit(solution)/shard_map/pallas_call | solution.py:380
  80.1 0.7 copy.12
  80.7 0.6 copy.13
  81.3 0.6 copy.14
Async XLA Ops:
  0.6 1.2 %copy-start = (bf16[168,3328]{1,0:T(8,128)(2,1)S(1)}, bf16[168,3328]{1,0:T(8,128)(2,1)}, u32[]{:S(2)}) copy-start(bf16[168,3328]{1,0:T(8,128)(2,1)} %hidden.1) | copy-start | bytes 3354628
  1.9 0.9 %copy-start.1 = (bf16[168,384]{1,0:T(8,128)(2,1)S(1)}, bf16[168,384]{1,0:T(8,128)(2,1)}, u32[]{:S(2)}) copy-start(bf16[168,384]{1,0:T(8,128)(2,1)} %down.1) | copy-start | bytes 387076
  2.8 0.9 %copy-start.2 = (bf16[128,384]{1,0:T(8,128)(2,1)S(1)}, bf16[128,384]{1,0:T(8,128)(2,1)}, u32[]{:S(2)}) copy-start(bf16[128,384]{1,0:T(8,128)(2,1)} %grad_out.1) | copy-start | bytes 294916
  3.7 0.7 copy-start.3
  4.4 0.7 copy-start.4
  5.1 0.7 copy-start.5

commit v2 on v1

v2 whole, which is shorter than its diff:
```python
import functools

import jax
import jax.numpy as jnp
from jax import lax
from jax.experimental import pallas as pl
from jax.experimental.pallas import tpu as pltpu
from jax.sharding import PartitionSpec as P

MESH = pl.DeviceIdType.MESH
CAP = 52
NZ, NX, NY = 16, 4, 8
PLAN = (
    (0, ((0, 0, 1), (0, 0, 3), (0, 0, 2), (2, -1, 0), (2, 1, 0))),
    (-1, ((2, -3, 0), (2, 3, 0), (1, -2, 0), (1, 2, 0), (1, -2, 1), (1, 2, 1), (1, -2, 3), (1, 2, 3), (1, -2, 2), (1, 2, 2), (2, -2, 0))),
    (1, ()),
    (-2, ((2, -4, 0), (2, 2, 0), (2, 4, 0), (2, -6, 0), (2, 6, 0), (1, -4, 0), (1, 4, 0), (1, -4, 1), (1, 4, 1))),
    (-3, ((1, -4, 3), (1, 4, 3), (1, -4, 2), (1, 4, 2), (2, -7, 0), (2, -5, 0), (2, 5, 0), (2, 7, 0))),
    (3, ()),
    (-4, ((1, -6, 0), (1, 6, 0), (1, -6, 1), (1, 6, 1))),
    (2, ((1, -6, 3), (1, 6, 3))),
    (4, ((1, -6, 2), (2, 8, 0), (1, 6, 2))),
    (-6, ()),
    (6, ()),
    (-5, ()),
    (-7, ()),
    (5, ()),
    (7, ()),
    (8, ()),
)
DZ = tuple(d for d, _ in PLAN)
AT = {d: i for i, d in enumerate(DZ)}
AT[-8] = AT[8]
HAND_A = {0: (2, -2, 1, -1), -2: (2, 1), 2: (-2, -1), -4: (2, 1), 4: (-2, -1), -6: (1, 2), 6: (-1,)}
HAND_B = {0: (3, -3, 1, -1), -3: (3, 1, -1), 3: (-3, 1, -1), -6: (1, -1), 6: (1, -1), -7: (1,)}
AHEAD = 5
F32, BF16 = jnp.float32, jnp.bfloat16


def pick(index, table):
    out = jnp.int32(table[0])
    for i, v in enumerate(table):
        if i:
            out = jnp.where(index == i, jnp.int32(v), out)
    return out


def pack(v):
    lane = lax.rem(lax.broadcasted_iota(jnp.int32, (144, 256), 1), 64)
    tail = [pltpu.roll(v[144:168], CAP - 12 * c, 1) for c in range(5)]
    tail.append(jnp.zeros((24, 256), F32))
    return jnp.where(lane < CAP, v[0:144], jnp.concatenate(tail, axis=0))


def unpack(v):
    lane = lax.rem(lax.broadcasted_iota(jnp.int32, (24, 256), 1), 64)
    tail = jnp.zeros((24, 256), F32)
    for c in range(5):
        part = pltpu.roll(v[24 * c:24 * c + 24], 256 - (CAP - 12 * c), 1)
        tail = jnp.where((lane >= 12 * c) & (lane < 12 * c + 12), part, tail)
    return jnp.concatenate([v, tail], axis=0)


def kernel(
    grad_out, logits_t, ids_t, hidden, down, router_t,
    grad_down, grad_hidden, grad_tokens,
    go_v, log_v, ids_v, hid_v, down_v, rw_v,
    hp, abuf, bbuf, acc, own, pbuf, sib, comb, rsb, wshare,
    sc, s1, s3s, s3, s4s, s4, sel_t, qmat,
    in_sem, ax_s, ax_r, az_s, az_r, bz_s, bz_r, bx_s, bx_r,
    sib_s, sib_r, y_s, y_r, s1_s, s1_r, s3_s, s3_r, s4_s, s4_r,
):
    ctx, ep = lax.axis_index("ctx"), lax.axis_index("ep")
    z, x = ctx // NX, lax.rem(ctx, NX)
    y, core = ep // 2, lax.rem(ep, 2)

    def at_z(d):
        return (lax.rem(z + d + NZ, NZ) * NX + x, ep)

    def at_x(d):
        return (z * NX + lax.rem(x + d, NX), ep)

    def at_y(d):
        return (ctx, lax.rem(y + d, NY) * 2 + core)

    def from_x(o):
        return lax.rem(x + NX - o, NX)

    sibling = (ctx, y * 2 + 1 - core)

    def remote(src, dst, send, recv, to):
        return pltpu.make_async_remote_copy(
            src_ref=src, dst_ref=dst, send_sem=send, recv_sem=recv, device_id=to, device_id_type=MESH
        )

    def arrived(ref, sem):
        remote(ref, ref, s4_s, sem, sibling).wait_recv()

    def sent(ref, sem):
        remote(ref, ref, sem, s4_r, sibling).wait_send()

    loads = [
        pltpu.make_async_copy(s, d, in_sem.at[i])
        for i, (s, d) in enumerate(
            ((ids_t, ids_v), (grad_out, go_v), (logits_t, log_v), (hidden, hid_v), (down, down_v), (router_t, rw_v))
        )
    ]
    for c in loads:
        c.start()

    barrier = pltpu.get_barrier_semaphore()
    greet = [at_z(d) for d in (1, -1, 2, -2, 3, -3)] + [at_x(d) for d in (1, 2, 3)]
    greet += [at_y(d) for d in range(1, NY)] + [sibling]
    for to in greet:
        pl.semaphore_signal(barrier, inc=1, device_id=to, device_id_type=MESH)

    loads[0].wait()
    named = jnp.max(jnp.where(ids_v[...] == 0, 1.0, 0.0).astype(F32), axis=0, keepdims=True)
    rows = lax.broadcasted_iota(jnp.int32, (128, 128), 0)
    cols = lax.broadcasted_iota(jnp.int32, (128, 128), 1)
    before = jnp.where(rows < cols, 1.0, 0.0).astype(BF16)
    named8 = jnp.broadcast_to(named, (8, 128))
    pos = jnp.dot(named8.astype(BF16), before, preferred_element_type=F32)[0:1]
    slot_row = lax.rem(rows, 64).astype(F32)
    sel = jnp.where((slot_row == pos) & (named > 0.5), 1.0, 0.0).astype(F32)
    sel_bf = sel.astype(BF16)

    loads[2].wait()
    logit = log_v[...]
    grown = jnp.exp(logit - jnp.max(logit, axis=0, keepdims=True))
    probs = grown / jnp.sum(grown, axis=0, keepdims=True)
    p0 = probs[0:1]
    weight = jnp.where(named > 0.5, p0, 0.0).astype(BF16)
    weight_row = lax.dot_general(
        jnp.broadcast_to(weight.astype(F32), (8, 128)).astype(BF16), sel_bf,
        (((1,), (1,)), ((), ())), preferred_element_type=F32,
    )[0:1]

    loads[1].wait()
    slots = jnp.dot(sel_bf[0:64], go_v[...], preferred_element_type=F32)[0:56]
    row56 = lax.broadcasted_iota(jnp.int32, (56, 128), 0)
    first = jnp.where(row56 == CAP, weight_row, slots[:, 0:128])
    abuf[0, x] = first.reshape(7, 8, 128).astype(BF16)
    bbuf[x, 0] = jnp.concatenate([slots[:, 128:256], slots[:, 256:384]], axis=0).astype(BF16)

    pl.semaphore_wait(barrier, len(greet))

    def leaf(d):
        return d not in HAND_A

    def send_a(d, o):
        k = from_x(o)
        for shift in HAND_A[d]:
            there = d - shift
            if there == -8:
                there = 8
            sem = az_r.at[AT[there], 0 if leaf(there) else o]
            remote(abuf.at[AT[d], k], abuf.at[AT[there], k], az_s, sem, at_z(shift)).start()

    def send_b(d):
        for shift in HAND_B.get(d, ()):
            there = AT[d - shift]
            remote(bbuf.at[x, AT[d]], bbuf.at[x, there], bz_s, bz_r.at[there], at_z(shift)).start()

    def send_bx(i):
        for o in (1, 3, 2):
            remote(bbuf.at[x, i], bbuf.at[x, i], bx_s, bx_r.at[i], at_x(o)).start()

    for o in (1, 3, 2):
        remote(abuf.at[0, x], abuf.at[0, x], ax_s, ax_r.at[o], at_x(o)).start()
    send_b(0)
    send_a(0, 0)
    send_bx(0)

    def hand_on(op, d, o):
        if op == 0:
            arrived(abuf.at[0, from_x(o)], ax_r.at[o])
            send_a(0, o)
        elif op == 1:
            arrived(abuf.at[AT[d], from_x(o)], az_r.at[AT[d], o])
            send_a(d, o)
        else:
            arrived(bbuf.at[x, AT[d]], bz_r.at[AT[d]])
            send_b(d)
            send_bx(AT[d])

    loads[3].wait()

    def share_of(i):
        return lax.rem(z + pick(i, DZ) + NZ, NZ)

    def spread(i, _):
        start = share_of(i) * (NX * CAP)
        tile = jnp.minimum(start // 128, 23)
        off = start - tile * 128
        r = lax.broadcasted_iota(jnp.int32, (384, 256), 0)
        c = lax.broadcasted_iota(jnp.int32, (384, 256), 1)
        lane = lax.rem(c, 64)
        move = jnp.where((r == off + (c // 64) * CAP + lane) & (lane < CAP), 1.0, 0.0).astype(BF16)
        out = jnp.dot(hid_v[:, pl.ds(pl.multiple_of(tile * 128, 128), 384)], move, preferred_element_type=F32)
        hp[i] = out.astype(BF16)
        return 0

    lax.fori_loop(0, AHEAD, spread, 0)
    acc[...] = jnp.zeros_like(acc)
    loads[4].wait()

    lane128 = lax.broadcasted_iota(jnp.int32, (1, 128), 1)

    def score_to(i, k):
        return remote(sc.at[i, k // 2], s1.at[i * NX + x], s1_s, s1_r, (share_of(i) * NX + k, ep))

    def add_pair(i):
        e = share_of(i)

        @pl.when(lax.rem(e, 2) == core)
        def _():
            arrived(sib.at[i], sib_r.at[i])
            both = (own[lax.rem(i, 2)] + sib[i].astype(F32)).astype(BF16)

            @pl.when(e == ep)
            def _():
                rsb[y] = both

            @pl.when(e != ep)
            def _():
                comb[i] = both
                remote(comb.at[i], rsb.at[y], y_s, y_r.at[y], (ctx, e)).start()

    def chunk(i):
        e = share_of(i)
        a = [abuf[i, k].astype(F32).reshape(56, 128) for k in range(NX)]
        b = [bbuf[k, i].astype(F32) for k in range(NX)]
        pad = jnp.zeros((8, 128), F32)
        g0 = jnp.concatenate([v for k in range(NX) for v in (a[k], pad)], axis=0).astype(BF16)
        g1 = jnp.concatenate([v for k in range(NX) for v in (b[k][0:56], pad)], axis=0).astype(BF16)
        g2 = jnp.concatenate([v for k in range(NX) for v in (b[k][56:112], pad)], axis=0).astype(BF16)
        g = jnp.concatenate([g0, g1, g2], axis=1)
        w = jnp.concatenate(
            [jnp.where(lane128 < 64, a[k][CAP:CAP + 1], a[k + 1][CAP:CAP + 1]) for k in (0, 2)], axis=1
        )
        h = hp[i].astype(F32)
        back = lax.dot_general(down_v[...], g, (((1,), (1,)), ((), ())), preferred_element_type=F32)
        score = jnp.sum(h * back, axis=0, keepdims=True)
        sc[i, 0] = score[:, 0:128]
        sc[i, 1] = score[:, 128:256]
        for k in range(NX):
            @pl.when((i != 0) | (x != k))
            def _(k=k):
                score_to(i, k).start()

        @pl.when(i == 0)
        def _():
            s1[x] = jnp.where(x >= 2, score[:, 128:256], score[:, 0:128])

        packed = pack(back)

        @pl.when(lax.rem(e, 2) == core)
        def _():
            own[lax.rem(i, 2)] = packed

        @pl.when(lax.rem(e, 2) != core)
        def _():
            pbuf[i] = packed.astype(BF16)
            remote(pbuf.at[i], sib.at[i], sib_s, sib_r.at[i], sibling).start()

        @pl.when(e == ep)
        def _():
            wshare[...] = jnp.broadcast_to(w, (8, 256))

        acc[...] += jnp.dot((h * w).astype(BF16), g, preferred_element_type=F32)

        @pl.when(i != 0)
        def _():
            add_pair(i - 1)

    def step(i, _):
        @pl.when(i < 16 - AHEAD)
        def _():
            spread(i + AHEAD, 0)

        for k, (d, ops) in enumerate(PLAN):
            @pl.when(i == k)
            def _(k=k, d=d, ops=ops):
                for op in ops:
                    hand_on(*op)
                if d != 0 and leaf(d):
                    arrived(abuf.at[k], az_r.at[k, 0])
                if k == 1:
                    sel_t[...] = sel.T
                    loads[5].wait()
                    top = lax.broadcasted_iota(jnp.int32, (16, 128), 0) == 0
                    qmat[...] = lax.dot_general(
                        probs * (jnp.where(top, 1.0, 0.0) - p0), rw_v[...], (((0,), (0,)), ((), ())),
                        precision=lax.Precision.HIGHEST, preferred_element_type=F32,
                    )

        arrived(bbuf.at[pl.ds(0, 3), i], bx_r.at[i])
        chunk(i)
        return 0

    lax.fori_loop(0, 16, step, 0)
    add_pair(15)

    arrived(s1.at[pl.ds(0, 63)], s1_r)
    s3s[...] = jnp.sum(s1[...], axis=0)
    for d in range(1, NY):
        remote(s3s, s3.at[d], s3_s, s3_r, at_y(d)).start()
    s3[0] = s3s[...]
    grad_down[...] = acc[...].astype(BF16)
    arrived(s3.at[pl.ds(0, NY - 1)], s3_r)
    s4s[...] = jnp.sum(s3[...], axis=0)
    last = remote(s4s, s4, s4_s, s4_r, sibling)
    last.start()

    for d in range(1, NY):
        src = lax.rem(y + NY - d, NY)
        arrived(rsb.at[src], y_r.at[src])
    total = rsb[0].astype(F32)
    for d in range(1, NY):
        total = total + rsb[d].astype(F32)
    total = unpack(total) * wshare[0:1]
    grad_hidden[...] = jnp.concatenate([total[:, 64 * k:64 * k + CAP] for k in range(NX)], axis=1).astype(BF16)

    last.wait()
    scores = s4s[...] + s4[...]
    row = jnp.where(lane128 // 64 == lax.rem(x, 2), scores, 0.0)
    route = jnp.sum(sel_t[...] * row, axis=1, keepdims=True)
    grad_tokens[...] = (route * qmat[...]).astype(BF16)

    sent(abuf.at[0, pl.ds(0, 3)], ax_s)
    sent(abuf.at[pl.ds(0, 15)], az_s)
    sent(bbuf.at[0, pl.ds(0, 15)], bz_s)
    sent(bbuf.at[pl.ds(0, 3)], bx_s)
    sent(pbuf.at[pl.ds(0, 8)], sib_s)
    sent(comb.at[pl.ds(0, 7)], y_s)
    sent(s1.at[pl.ds(0, 63)], s1_s)
    sent(s3.at[pl.ds(0, NY - 1)], s3_s)


def shards(grad_out, logits, expert_ids, hidden_act, down_weight, router_weight):
    dma = pltpu.SemaphoreType.DMA
    return pl.pallas_call(
        kernel,
        out_shape=(
            jax.ShapeDtypeStruct((168, 384), BF16),
            jax.ShapeDtypeStruct((168, 208), BF16),
            jax.ShapeDtypeStruct((128, 384), BF16),
        ),
        in_specs=[pl.BlockSpec(memory_space=pl.ANY)] * 6,
        out_specs=[pl.BlockSpec(memory_space=pltpu.VMEM)] * 3,
        scratch_shapes=[
            pltpu.VMEM((128, 384), BF16),
            pltpu.VMEM((16, 128), F32),
            pltpu.VMEM((4, 128), jnp.int32),
            pltpu.VMEM((168, 3328), BF16),
            pltpu.VMEM((168, 384), BF16),
            pltpu.VMEM((16, 384), F32),
            pltpu.VMEM((16, 168, 256), BF16),
            pltpu.VMEM((16, NX, 7, 8, 128), BF16),
            pltpu.VMEM((NX, 16, 112, 128), BF16),
            pltpu.VMEM((168, 384), F32),
            pltpu.VMEM((2, 144, 256), F32),
            pltpu.VMEM((16, 144, 256), BF16),
            pltpu.VMEM((16, 144, 256), BF16),
            pltpu.VMEM((16, 144, 256), BF16),
            pltpu.VMEM((NY, 144, 256), BF16),
            pltpu.VMEM((8, 256), F32),
            pltpu.VMEM((16, 2, 1, 128), F32),
            pltpu.VMEM((64, 1, 128), F32),
            pltpu.VMEM((1, 128), F32),
            pltpu.VMEM((NY, 1, 128), F32),
            pltpu.VMEM((1, 128), F32),
            pltpu.VMEM((1, 128), F32),
            pltpu.VMEM((128, 128), F32),
            pltpu.VMEM((128, 384), F32),
            dma((6,)),
            dma, dma((NX,)),
            dma, dma((16, NX)),
            dma, dma((16,)),
            dma, dma((16,)),
            dma, dma((16,)),
            dma, dma((NY,)),
            dma, dma,
            dma, dma,
            dma, dma,
        ],
        compiler_params=pltpu.CompilerParams(
            collective_id=0, has_side_effects=True, vmem_limit_bytes=56 << 20
        ),
    )(grad_out, logits.T, expert_ids.T, hidden_act, down_weight, router_weight.T)


def solution(mesh):
    placed = (
        P("ctx", "ep"),
        P("ctx", None),
        P("ctx", None),
        P("ctx", None),
        P("ctx", "ep"),
        P("ep", None),
    )
    return jax.shard_map(
        shards,
        mesh=mesh,
        in_specs=placed,
        out_specs=(P("ctx", "ep"), P("ctx", "ep"), P("ctx", "ep")),
        check_vma=False,
    )
```

time: 82.3 us -> 72.1 us (0.88)
  Pallas kernels: 74.2 us -> 66.5 us
  local copies, waits for them, and re-layouts: 7.08 us -> 4.64 us
    pallas_call x1, Pallas kernels: 74.2 us -> 66.5 us  [shards(): pl.pallas_call(kernel, out_shape=(jax.ShapeDtypeStruct((168, 384), BF16),...]
    unnamed x15 -> x3, local copies, waits for them, and re-layouts: 7.08 us -> 4.64 us
where the time goes in v2:
time: 72.1 us; the launch traced here: 71.8 us
  Pallas kernels  66.5 us (92%)
  local copies, waits for them, and re-layouts  4.64 us (6%)
    pallas_call x1, Pallas kernels, shards(): pl.pallas_call(kernel, out_shape=(jax.ShapeDtypeStruct((168, 384), BF16),...  66.5 us
    unnamed x3, local copies, waits for them, and re-layouts  4.64 us

profile of v2, /device:TPU:1, one launch (start us, length us, event | category | flops | bytes accessed | tf_op | source)
XLA Modules:
  0.0 71.8 jit_solution(17042642668762729956)
XLA Ops:
  0.6 66.5 %shard_map.85 = (bf16[168,384]{1,0:T(8,128)(2,1)}, bf16[168,208]{1,0:T(8,128)(2,1)}, bf16[128,384]{1,0:T(8,128)(2,1)}) custom-call(bf16[128,384]{1,0:T(8,128)(2,1)} %grad_out.1, f32[16,128]{1,0:T(8,128)} %bitcast.4, s32[4,128]{1,0:T(4,128)} %bitcast.5, bf16[168,3328]{1,0:T(8,128)(2,1)} %hidden.1, bf16[168,384]{1,0:T(8,128)(2,1)} %down.1, f32[16,384]{1,0:T(8,128)} %bitcast.3), custom_call_target="tpu_custom_call" | custom-call | tf_op jit(solution)/shard_map/pallas_call | solution.py:343
  67.2 1.6 %copy.12 = bf16[168,384]{1,0:T(8,128)(2,1)} copy(bf16[168,384]{1,0:T(8,128)(2,1)} %get-tuple-element.6) | data formatting | bytes 258048
  68.7 1.5 %copy.13 = bf16[168,208]{1,0:T(8,128)(2,1)} copy(bf16[168,208]{1,0:T(8,128)(2,1)} %get-tuple-element.7) | data formatting | bytes 139776
  70.3 1.5 %copy.14 = bf16[128,384]{1,0:T(8,128)(2,1)} copy(bf16[128,384]{1,0:T(8,128)(2,1)} %get-tuple-element.8) | data formatting | bytes 196608

commit v3 on v2

--- a/solution.py
+++ b/solution.py
@@ -11,28 +11,27 @@
 CAP = 52
 NZ, NX, NY = 16, 4, 8
 PLAN = (
-    (0, ((0, 0, 1), (0, 0, 3), (0, 0, 2), (2, -1, 0), (2, 1, 0))),
-    (-1, ((2, -3, 0), (2, 3, 0), (1, -2, 0), (1, 2, 0), (1, -2, 1), (1, 2, 1), (1, -2, 3), (1, 2, 3), (1, -2, 2), (1, 2, 2), (2, -2, 0))),
-    (1, ()),
-    (-2, ((2, -4, 0), (2, 2, 0), (2, 4, 0), (2, -6, 0), (2, 6, 0), (1, -4, 0), (1, 4, 0), (1, -4, 1), (1, 4, 1))),
-    (-3, ((1, -4, 3), (1, 4, 3), (1, -4, 2), (1, 4, 2), (2, -7, 0), (2, -5, 0), (2, 5, 0), (2, 7, 0))),
-    (3, ()),
-    (-4, ((1, -6, 0), (1, 6, 0), (1, -6, 1), (1, 6, 1))),
-    (2, ((1, -6, 3), (1, 6, 3))),
-    (4, ((1, -6, 2), (2, 8, 0), (1, 6, 2))),
-    (-6, ()),
+    (0, ((0, 0, 1), (0, 0, 3), (0, 0, 2), (2, -1, 0), (2, 1, 0), (2, -2, 0), (2, 2, 0))),
+    (-1, ((1, -2, 0), (1, 2, 0), (1, -2, 1), (1, 2, 1), (1, -2, 3), (1, 2, 3), (1, -2, 2), (1, 2, 2))),
+    (1, ((2, -3, 0), (2, 3, 0), (2, -4, 0), (2, 4, 0))),
+    (-2, ((1, -4, 0), (1, 4, 0), (1, -4, 1), (1, 4, 1))),
+    (2, ((1, -4, 3), (1, 4, 3))),
+    (-3, ((1, -4, 2), (1, 4, 2))),
+    (3, ((2, -5, 0), (2, -6, 0), (2, 5, 0), (2, 6, 0), (1, -6, 0), (1, 6, 0))),
+    (-4, ((1, -6, 1), (1, 6, 1))),
+    (4, ((1, -6, 3), (1, 6, 3), (1, -6, 2), (1, 6, 2), (2, -7, 0))),
+    (-5, ((2, 7, 0),)),
+    (-6, ((2, 8, 0),)),
+    (5, ()),
     (6, ()),
-    (-5, ()),
     (-7, ()),
-    (5, ()),
     (7, ()),
     (8, ()),
 )
 DZ = tuple(d for d, _ in PLAN)
 AT = {d: i for i, d in enumerate(DZ)}
 AT[-8] = AT[8]
-HAND_A = {0: (2, -2, 1, -1), -2: (2, 1), 2: (-2, -1), -4: (2, 1), 4: (-2, -1), -6: (1, 2), 6: (-1,)}
-HAND_B = {0: (3, -3, 1, -1), -3: (3, 1, -1), 3: (-3, 1, -1), -6: (1, -1), 6: (1, -1), -7: (1,)}
+HAND = {0: (2, -2, 1, -1), -2: (2, 1), 2: (-2, -1), -4: (2, 1), 4: (-2, -1), -6: (1, 2), 6: (-1,)}
 AHEAD = 5
 F32, BF16 = jnp.float32, jnp.bfloat16
 
@@ -66,9 +65,9 @@
     grad_down, grad_hidden, grad_tokens,
     go_v, log_v, ids_v, hid_v, down_v, rw_v,
     hp, abuf, bbuf, acc, own, pbuf, sib, comb, rsb, wshare,
-    sc, s1, s3s, s3, s4s, s4, sel_t, qmat,
+    sc, s1, s3s, s3, sel_t, qmat,
     in_sem, ax_s, ax_r, az_s, az_r, bz_s, bz_r, bx_s, bx_r,
-    sib_s, sib_r, y_s, y_r, s1_s, s1_r, s3_s, s3_r, s4_s, s4_r,
+    sib_s, sib_r, y_s, y_r, s1_s, s1_r, s3_s, s3_r, known,
 ):
     ctx, ep = lax.axis_index("ctx"), lax.axis_index("ep")
     z, x = ctx // NX, lax.rem(ctx, NX)
@@ -94,10 +93,10 @@
         )
 
     def arrived(ref, sem):
-        remote(ref, ref, s4_s, sem, sibling).wait_recv()
+        remote(ref, ref, s3_s, sem, sibling).wait_recv()
 
     def sent(ref, sem):
-        remote(ref, ref, sem, s4_r, sibling).wait_send()
+        remote(ref, ref, sem, s3_r, sibling).wait_send()
 
     loads = [
         pltpu.make_async_copy(s, d, in_sem.at[i])
@@ -109,8 +108,8 @@
         c.start()
 
     barrier = pltpu.get_barrier_semaphore()
-    greet = [at_z(d) for d in (1, -1, 2, -2, 3, -3)] + [at_x(d) for d in (1, 2, 3)]
-    greet += [at_y(d) for d in range(1, NY)] + [sibling]
+    greet = [at_z(d) for d in (2, -2, 1, -1)] + [at_x(d) for d in (2, 1, 3)]
+    greet += [at_y(1), at_y(NY - 1), sibling]
     for to in greet:
         pl.semaphore_signal(barrier, inc=1, device_id=to, device_id_type=MESH)
 
@@ -145,12 +144,19 @@
 
     pl.semaphore_wait(barrier, len(greet))
 
+    def pass_on(hop):
+        if hop > 1:
+            pl.semaphore_wait(known.at[hop - 2], 2)
+        if hop < NY // 2:
+            for to in (at_y(1), at_y(NY - 1)):
+                pl.semaphore_signal(known.at[hop - 1], inc=1, device_id=to, device_id_type=MESH)
+
     def leaf(d):
-        return d not in HAND_A
+        return d not in HAND
 
     def send_a(d, o):
         k = from_x(o)
-        for shift in HAND_A[d]:
+        for shift in HAND[d]:
             there = d - shift
             if there == -8:
                 there = 8
@@ -158,7 +164,7 @@
             remote(abuf.at[AT[d], k], abuf.at[AT[there], k], az_s, sem, at_z(shift)).start()
 
     def send_b(d):
-        for shift in HAND_B.get(d, ()):
+        for shift in HAND.get(d, ()):
             there = AT[d - shift]
             remote(bbuf.at[x, AT[d]], bbuf.at[x, there], bz_s, bz_r.at[there], at_z(shift)).start()
 
@@ -171,6 +177,7 @@
     send_b(0)
     send_a(0, 0)
     send_bx(0)
+    pass_on(1)
 
     def hand_on(op, d, o):
         if op == 0:
@@ -282,11 +289,14 @@
         for k, (d, ops) in enumerate(PLAN):
             @pl.when(i == k)
             def _(k=k, d=d, ops=ops):
-                for op in ops:
+                for n, op in enumerate(ops):
+                    if k < 2 and n == 3:
+                        pass_on(k + 2)
                     hand_on(*op)
                 if d != 0 and leaf(d):
                     arrived(abuf.at[k], az_r.at[k, 0])
                 if k == 1:
+                    pass_on(4)
                     sel_t[...] = sel.T
                     loads[5].wait()
                     top = lax.broadcasted_iota(jnp.int32, (16, 128), 0) == 0
@@ -304,14 +314,13 @@
 
     arrived(s1.at[pl.ds(0, 63)], s1_r)
     s3s[...] = jnp.sum(s1[...], axis=0)
-    for d in range(1, NY):
-        remote(s3s, s3.at[d], s3_s, s3_r, at_y(d)).start()
+    for d in (4, 3, 5, 2, 6, 1, 7, 0):
+        for other in (0, 1):
+            if d or other:
+                to = (ctx, lax.rem(y + d, NY) * 2 + (1 - core if other else core))
+                remote(s3s, s3.at[2 * d + other], s3_s, s3_r, to).start()
     s3[0] = s3s[...]
     grad_down[...] = acc[...].astype(BF16)
-    arrived(s3.at[pl.ds(0, NY - 1)], s3_r)
-    s4s[...] = jnp.sum(s3[...], axis=0)
-    last = remote(s4s, s4, s4_s, s4_r, sibling)
-    last.start()
 
     for d in range(1, NY):
         src = lax.rem(y + NY - d, NY)
@@ -322,9 +331,8 @@
     total = unpack(total) * wshare[0:1]
     grad_hidden[...] = jnp.concatenate([total[:, 64 * k:64 * k + CAP] for k in range(NX)], axis=1).astype(BF16)
 
-    last.wait()
-    scores = s4s[...] + s4[...]
-    row = jnp.where(lane128 // 64 == lax.rem(x, 2), scores, 0.0)
+    arrived(s3.at[pl.ds(0, 15)], s3_r)
+    row = jnp.where(lane128 // 64 == lax.rem(x, 2), jnp.sum(s3[...], axis=0), 0.0)
     route = jnp.sum(sel_t[...] * row, axis=1, keepdims=True)
     grad_tokens[...] = (route * qmat[...]).astype(BF16)
 
@@ -335,17 +343,27 @@
     sent(pbuf.at[pl.ds(0, 8)], sib_s)
     sent(comb.at[pl.ds(0, 7)], y_s)
     sent(s1.at[pl.ds(0, 63)], s1_s)
-    sent(s3.at[pl.ds(0, NY - 1)], s3_s)
+    sent(s3.at[pl.ds(0, 15)], s3_s)
+
+
+def copy_out(a, b, c, a_out, b_out, c_out, sem):
+    copies = [
+        pltpu.make_async_copy(v, o, sem.at[i]) for i, (v, o) in enumerate(((a, a_out), (b, b_out), (c, c_out)))
+    ]
+    for v in copies:
+        v.start()
+    for v in copies:
+        v.wait()
 
 
 def shards(grad_out, logits, expert_ids, hidden_act, down_weight, router_weight):
     dma = pltpu.SemaphoreType.DMA
-    return pl.pallas_call(
+    results = pl.pallas_call(
         kernel,
         out_shape=(
-            jax.ShapeDtypeStruct((168, 384), BF16),
-            jax.ShapeDtypeStruct((168, 208), BF16),
-            jax.ShapeDtypeStruct((128, 384), BF16),
+            pltpu.VMEM((168, 384), BF16),
+            pltpu.VMEM((168, 208), BF16),
+            pltpu.VMEM((128, 384), BF16),
         ),
         in_specs=[pl.BlockSpec(memory_space=pl.ANY)] * 6,
         out_specs=[pl.BlockSpec(memory_space=pltpu.VMEM)] * 3,
@@ -369,9 +387,7 @@
             pltpu.VMEM((16, 2, 1, 128), F32),
             pltpu.VMEM((64, 1, 128), F32),
             pltpu.VMEM((1, 128), F32),
-            pltpu.VMEM((NY, 1, 128), F32),
-            pltpu.VMEM((1, 128), F32),
-            pltpu.VMEM((1, 128), F32),
+            pltpu.VMEM((16, 1, 128), F32),
             pltpu.VMEM((128, 128), F32),
             pltpu.VMEM((128, 384), F32),
             dma((6,)),
@@ -383,12 +399,19 @@
             dma, dma((NY,)),
             dma, dma,
             dma, dma,
-            dma, dma,
+            pltpu.SemaphoreType.REGULAR((3,)),
         ],
         compiler_params=pltpu.CompilerParams(
             collective_id=0, has_side_effects=True, vmem_limit_bytes=56 << 20
         ),
     )(grad_out, logits.T, expert_ids.T, hidden_act, down_weight, router_weight.T)
+    return pl.pallas_call(
+        copy_out,
+        out_shape=tuple(jax.ShapeDtypeStruct(r.shape, r.dtype) for r in results),
+        in_specs=[pl.BlockSpec(memory_space=pltpu.VMEM)] * 3,
+        out_specs=[pl.BlockSpec(memory_space=pl.ANY)] * 3,
+        scratch_shapes=[dma((3,))],
+    )(*(pltpu.with_memory_space_constraint(r, pltpu.VMEM) for r in results))
 
 
 def solution(mesh):

time: 72.1 us -> 63.9 us (0.89)
  local copies, waits for them, and re-layouts: 4.64 us -> 0 us
  Pallas kernels: 66.5 us -> 63.1 us
    unnamed x3 -> x0, local copies, waits for them, and re-layouts: 4.64 us -> none
    pallas_call x1 -> x2, Pallas kernels: 66.5 us -> 63.1 us  [the longest x1 62.3 us: shards(): pl.pallas_call(kernel, out_shape=(pltpu.VMEM((168, 384), BF16), pltpu.VME...]
where the time goes in v3:
time: 63.9 us; the launch traced here: 63.7 us
  Pallas kernels  63.1 us (99%)
  between operations  0.64 us (1%)
    pallas_call x1, Pallas kernels, shards(): pl.pallas_call(kernel, out_shape=(pltpu.VMEM((168, 384), BF16), pltpu.VME...  62.3 us

profile of v3, /device:TPU:1, one launch (start us, length us, event | category | flops | bytes accessed | tf_op | source)
XLA Modules:
  0.0 63.7 jit_solution(3372471786761866601)
XLA Ops:
  0.6 62.3 %shard_map.85 = (bf16[168,384]{1,0:T(8,128)(2,1)S(1)}, bf16[168,208]{1,0:T(8,128)(2,1)S(1)}, bf16[128,384]{1,0:T(8,128)(2,1)S(1)}) custom-call(bf16[128,384]{1,0:T(8,128)(2,1)} %grad_out.1, f32[16,128]{1,0:T(8,128)} %bitcast.4, s32[4,128]{1,0:T(4,128)} %bitcast.5, bf16[168,3328]{1,0:T(8,128)(2,1)} %hidden.1, bf16[168,384]{1,0:T(8,128)(2,1)} %down.1, ...), custom_call_target="tpu_custom_call" | custom-call | tf_op jit(solution)/shard_map/pallas_call | solution.py:361
  63.0 0.7 %shard_map.86 = (bf16[168,384]{1,0:T(8,128)(2,1)}, bf16[168,208]{1,0:T(8,128)(2,1)}, bf16[128,384]{1,0:T(8,128)(2,1)}) custom-call(bf16[168,384]{1,0:T(8,128)(2,1)S(1)} %get-tuple-element.6.a, bf16[168,208]{1,0:T(8,128)(2,1)S(1)} %get-tuple-element.7.b, bf16[128,384]{1,0:T(8,128)(2,1)S(1)} %get-tuple-element.8.c), custom_call_target="tpu_custom_call" | custom-call | tf_op jit(solution)/shard_map/pallas_call | solution.py:408

commit v4 on v3

--- a/solution.py
+++ b/solution.py
@@ -15,15 +15,15 @@
     (-1, ((1, -2, 0), (1, 2, 0), (1, -2, 1), (1, 2, 1), (1, -2, 3), (1, 2, 3), (1, -2, 2), (1, 2, 2))),
     (1, ((2, -3, 0), (2, 3, 0), (2, -4, 0), (2, 4, 0))),
     (-2, ((1, -4, 0), (1, 4, 0), (1, -4, 1), (1, 4, 1))),
-    (2, ((1, -4, 3), (1, 4, 3))),
-    (-3, ((1, -4, 2), (1, 4, 2))),
-    (3, ((2, -5, 0), (2, -6, 0), (2, 5, 0), (2, 6, 0), (1, -6, 0), (1, 6, 0))),
-    (-4, ((1, -6, 1), (1, 6, 1))),
-    (4, ((1, -6, 3), (1, 6, 3), (1, -6, 2), (1, 6, 2), (2, -7, 0))),
-    (-5, ((2, 7, 0),)),
+    (2, ((1, -4, 3), (1, 4, 3), (1, -4, 2), (1, 4, 2))),
+    (-3, ((2, -5, 0),)),
+    (-4, ((2, -6, 0), (2, 5, 0), (2, 6, 0), (1, -6, 0), (1, 6, 0), (1, -6, 1), (1, 6, 1))),
+    (4, ((1, -6, 3), (1, 6, 3))),
+    (-5, ((1, -6, 2), (1, 6, 2), (2, -7, 0), (2, 7, 0))),
     (-6, ((2, 8, 0),)),
     (5, ()),
     (6, ()),
+    (3, ()),
     (-7, ()),
     (7, ()),
     (8, ()),
@@ -140,7 +140,11 @@
     row56 = lax.broadcasted_iota(jnp.int32, (56, 128), 0)
     first = jnp.where(row56 == CAP, weight_row, slots[:, 0:128])
     abuf[0, x] = first.reshape(7, 8, 128).astype(BF16)
-    bbuf[x, 0] = jnp.concatenate([slots[:, 128:256], slots[:, 256:384]], axis=0).astype(BF16)
+    rest = jnp.zeros((48, 128), F32)
+    upper = jnp.concatenate([slots[:, 128:256], rest], axis=0)
+    lower = pltpu.roll(jnp.concatenate([slots[:, 256:384], rest], axis=0), CAP, 0)
+    row104 = lax.broadcasted_iota(jnp.int32, (104, 128), 0)
+    bbuf[x, 0] = jnp.where(row104 < CAP, upper, lower).reshape(13, 8, 128).astype(BF16)
 
     pl.semaphore_wait(barrier, len(greet))
 
@@ -214,12 +218,10 @@
 
     lane128 = lax.broadcasted_iota(jnp.int32, (1, 128), 1)
 
-    def score_to(i, k):
-        return remote(sc.at[i, k // 2], s1.at[i * NX + x], s1_s, s1_r, (share_of(i) * NX + k, ep))
-
-    def add_pair(i):
-        e = share_of(i)
-
+    def score_to(i, e, k):
+        return remote(sc.at[i, k // 2], s1.at[i * NX + x], s1_s, s1_r, (e * NX + k, ep))
+
+    def add_pair(i, e):
         @pl.when(lax.rem(e, 2) == core)
         def _():
             arrived(sib.at[i], sib_r.at[i])
@@ -234,14 +236,14 @@
                 comb[i] = both
                 remote(comb.at[i], rsb.at[y], y_s, y_r.at[y], (ctx, e)).start()
 
-    def chunk(i):
-        e = share_of(i)
+    def chunk(i, e, before):
         a = [abuf[i, k].astype(F32).reshape(56, 128) for k in range(NX)]
-        b = [bbuf[k, i].astype(F32) for k in range(NX)]
+        b = [bbuf[k, i].astype(F32).reshape(104, 128) for k in range(NX)]
+        c = [pltpu.roll(v, CAP, 0) for v in b]
         pad = jnp.zeros((8, 128), F32)
         g0 = jnp.concatenate([v for k in range(NX) for v in (a[k], pad)], axis=0).astype(BF16)
         g1 = jnp.concatenate([v for k in range(NX) for v in (b[k][0:56], pad)], axis=0).astype(BF16)
-        g2 = jnp.concatenate([v for k in range(NX) for v in (b[k][56:112], pad)], axis=0).astype(BF16)
+        g2 = jnp.concatenate([v for k in range(NX) for v in (c[k][0:56], pad)], axis=0).astype(BF16)
         g = jnp.concatenate([g0, g1, g2], axis=1)
         w = jnp.concatenate(
             [jnp.where(lane128 < 64, a[k][CAP:CAP + 1], a[k + 1][CAP:CAP + 1]) for k in (0, 2)], axis=1
@@ -254,7 +256,7 @@
         for k in range(NX):
             @pl.when((i != 0) | (x != k))
             def _(k=k):
-                score_to(i, k).start()
+                score_to(i, e, k).start()
 
         @pl.when(i == 0)
         def _():
@@ -275,13 +277,13 @@
         def _():
             wshare[...] = jnp.broadcast_to(w, (8, 256))
 
+        @pl.when(i != 0)
+        def _():
+            add_pair(i - 1, before)
+
         acc[...] += jnp.dot((h * w).astype(BF16), g, preferred_element_type=F32)
 
-        @pl.when(i != 0)
-        def _():
-            add_pair(i - 1)
-
-    def step(i, _):
+    def step(i, before):
         @pl.when(i < 16 - AHEAD)
         def _():
             spread(i + AHEAD, 0)
@@ -306,11 +308,12 @@
                     )
 
         arrived(bbuf.at[pl.ds(0, 3), i], bx_r.at[i])
-        chunk(i)
-        return 0
-
-    lax.fori_loop(0, 16, step, 0)
-    add_pair(15)
+        e = share_of(i)
+        chunk(i, e, before)
+        return e
+
+    final = lax.fori_loop(0, 16, step, jnp.int32(0))
+    add_pair(15, final)
 
     arrived(s1.at[pl.ds(0, 63)], s1_r)
     s3s[...] = jnp.sum(s1[...], axis=0)
@@ -376,7 +379,7 @@
             pltpu.VMEM((16, 384), F32),
             pltpu.VMEM((16, 168, 256), BF16),
             pltpu.VMEM((16, NX, 7, 8, 128), BF16),
-            pltpu.VMEM((NX, 16, 112, 128), BF16),
+            pltpu.VMEM((NX, 16, 13, 8, 128), BF16),
             pltpu.VMEM((168, 384), F32),
             pltpu.VMEM((2, 144, 256), F32),
             pltpu.VMEM((16, 144, 256), BF16),

time: 63.9 us -> 62.9 us (0.984)
  Pallas kernels: 63.1 us -> 62.1 us
    pallas_call x1, Pallas kernels: 62.3 us -> 61.3 us  [shards(): pl.pallas_call(kernel, out_shape=(pltpu.VMEM((168, 384), BF16), pltpu.VME...]
where the time goes in v4:
time: 62.9 us; the launch traced here: 62.7 us
  Pallas kernels  62.1 us (99%)
  between operations  0.64 us (1%)
    pallas_call x1, Pallas kernels, shards(): pl.pallas_call(kernel, out_shape=(pltpu.VMEM((168, 384), BF16), pltpu.VME...  61.3 us

profile of v4, /device:TPU:1, one launch (start us, length us, event | category | flops | bytes accessed | tf_op | source)
XLA Modules:
  0.0 62.7 jit_solution(8919906098054288374)
XLA Ops:
  0.6 61.3 %shard_map.85 = (bf16[168,384]{1,0:T(8,128)(2,1)S(1)}, bf16[168,208]{1,0:T(8,128)(2,1)S(1)}, bf16[128,384]{1,0:T(8,128)(2,1)S(1)}) custom-call(bf16[128,384]{1,0:T(8,128)(2,1)} %grad_out.1, f32[16,128]{1,0:T(8,128)} %bitcast.4, s32[4,128]{1,0:T(4,128)} %bitcast.5, bf16[168,3328]{1,0:T(8,128)(2,1)} %hidden.1, bf16[168,384]{1,0:T(8,128)(2,1)} %down.1, ...), custom_call_target="tpu_custom_call" | custom-call | tf_op jit(solution)/shard_map/pallas_call | solution.py:364
  62.0 0.7 %shard_map.86 = (bf16[168,384]{1,0:T(8,128)(2,1)}, bf16[168,208]{1,0:T(8,128)(2,1)}, bf16[128,384]{1,0:T(8,128)(2,1)}) custom-call(bf16[168,384]{1,0:T(8,128)(2,1)S(1)} %get-tuple-element.6.a, bf16[168,208]{1,0:T(8,128)(2,1)S(1)} %get-tuple-element.7.b, bf16[128,384]{1,0:T(8,128)(2,1)S(1)} %get-tuple-element.8.c), custom_call_target="tpu_custom_call" | custom-call | tf_op jit(solution)/shard_map/pallas_call | solution.py:411

commit v5 on v4

--- a/solution.py
+++ b/solution.py
@@ -45,14 +45,14 @@
 
 
 def pack(v):
-    lane = lax.rem(lax.broadcasted_iota(jnp.int32, (144, 256), 1), 64)
+    lane = jnp.broadcast_to(lax.rem(lax.broadcasted_iota(jnp.int32, (1, 256), 1), 64), (144, 256))
     tail = [pltpu.roll(v[144:168], CAP - 12 * c, 1) for c in range(5)]
     tail.append(jnp.zeros((24, 256), F32))
     return jnp.where(lane < CAP, v[0:144], jnp.concatenate(tail, axis=0))
 
 
 def unpack(v):
-    lane = lax.rem(lax.broadcasted_iota(jnp.int32, (24, 256), 1), 64)
+    lane = jnp.broadcast_to(lax.rem(lax.broadcasted_iota(jnp.int32, (1, 256), 1), 64), (24, 256))
     tail = jnp.zeros((24, 256), F32)
     for c in range(5):
         part = pltpu.roll(v[24 * c:24 * c + 24], 256 - (CAP - 12 * c), 1)
@@ -205,9 +205,10 @@
         tile = jnp.minimum(start // 128, 23)
         off = start - tile * 128
         r = lax.broadcasted_iota(jnp.int32, (384, 256), 0)
-        c = lax.broadcasted_iota(jnp.int32, (384, 256), 1)
+        c = lax.broadcasted_iota(jnp.int32, (1, 256), 1)
         lane = lax.rem(c, 64)
-        move = jnp.where((r == off + (c // 64) * CAP + lane) & (lane < CAP), 1.0, 0.0).astype(BF16)
+        wanted = jnp.where(lane < CAP, off + (c // 64) * CAP + lane, -1)
+        move = jnp.where(r == wanted, 1.0, 0.0).astype(BF16)
         out = jnp.dot(hid_v[:, pl.ds(pl.multiple_of(tile * 128, 128), 384)], move, preferred_element_type=F32)
         hp[i] = out.astype(BF16)
         return 0

time: 62.9 us -> 62.9 us (level)
  no operation moved by 1% of the time
where the time goes in v5:
time: 62.9 us; the launch traced here: 62.7 us
  Pallas kernels  62.1 us (99%)
  between operations  0.64 us (1%)
    pallas_call x1, Pallas kernels, shards(): pl.pallas_call(kernel, out_shape=(pltpu.VMEM((168, 384), BF16), pltpu.VME...  61.3 us

profile of v5, /device:TPU:1, one launch (start us, length us, event | category | flops | bytes accessed | tf_op | source)
XLA Modules:
  0.0 62.7 jit_solution(4861880201284856956)
XLA Ops:
  0.6 61.3 %shard_map.85 = (bf16[168,384]{1,0:T(8,128)(2,1)S(1)}, bf16[168,208]{1,0:T(8,128)(2,1)S(1)}, bf16[128,384]{1,0:T(8,128)(2,1)S(1)}) custom-call(bf16[128,384]{1,0:T(8,128)(2,1)} %grad_out.1, f32[16,128]{1,0:T(8,128)} %bitcast.4, s32[4,128]{1,0:T(4,128)} %bitcast.5, bf16[168,3328]{1,0:T(8,128)(2,1)} %hidden.1, bf16[168,384]{1,0:T(8,128)(2,1)} %down.1, ...), custom_call_target="tpu_custom_call" | custom-call | tf_op jit(solution)/shard_map/pallas_call | solution.py:365
  62.0 0.7 %shard_map.86 = (bf16[168,384]{1,0:T(8,128)(2,1)}, bf16[168,208]{1,0:T(8,128)(2,1)}, bf16[128,384]{1,0:T(8,128)(2,1)}) custom-call(bf16[168,384]{1,0:T(8,128)(2,1)S(1)} %get-tuple-element.6.a, bf16[168,208]{1,0:T(8,128)(2,1)S(1)} %get-tuple-element.7.b, bf16[128,384]{1,0:T(8,128)(2,1)S(1)} %get-tuple-element.8.c), custom_call_target="tpu_custom_call" | custom-call | tf_op jit(solution)/shard_map/pallas_call | solution.py:412
